TPU v7x, 32 devices: a whole 2x2x4 slice. The times are simulated.
32 devices in a mesh: seq: 8 (over z, y), section: 4 (over x, core).
Axes of the slice: x: 2, y: 2, z: 4, core: 2. Of those that a mesh axis runs over, the one named last changes fastest.
Arguments:
- block_input: bfloat16 [4, 2048, 512], P('section', 'seq'), may hold values from -8 to 8
- upstream: bfloat16 [4, 2048, 512], P('section', 'seq'), may hold values from -6 to 6
- w_qkv: bfloat16 [4, 512, 768], P('section'), may hold values from -2 to 2
- w_out: bfloat16 [4, 256, 512], P('section'), may hold values from -0.375 to 0.375
- layer_norm_gain: float32 [4, 512], P('section'), may hold values from 0.1 to 1.9
- layer_norm_bias: float32 [4, 512], P('section'), may hold values from -3 to 3
- send_order: int32 [4, 8, 256], P('section', 'seq'), may hold values from 0 to 255, each once within a row
- recv_order: int32 [4, 8, 256], P('section', 'seq'), may hold values from 0 to 255, each once within a row
- patch_lengths: int32 [4, 8, 2], P('section', 'seq'), may hold values from 1 to 224, 256 in all within a row
Outputs:
- handed: bfloat16 [4, 2048, 512], P('section', 'seq')
Inputs may be any that keep to these rules, and one draw needn't show every extreme that they name: `send_order`: each device's row is a permutation of 0 to 255. `recv_order`: each device's row is a permutation of 0 to 255. `patch_lengths`: each device's lengths sum to 256; the largest is at most 224.
All inputs are finite; a program needn't handle non-finite values.
Results may differ from a plain program's by a relative error of at most 0.009.
The roundings to bfloat16 on the way count: a program that leaves them out, or rounds other values in their place, can miss the bound.
Values may be sent and summed in bfloat16 or wider, within the bound.
A program may use at most 64 MiB of HBM per device.

v0:
```python
import jax
import jax.numpy as jnp
from jax import lax
from jax.sharding import PartitionSpec as P

HEAD = 16


def from_behind(array, axis, by):
    peers = lax.axis_size(axis)
    pairs = [(i, i + by) for i in range(peers) if 0 <= i + by < peers]
    return lax.ppermute(array, axis, pairs)


def layer_normalize(rows, gain_weight, shift_bias):
    values = rows.astype(jnp.float32)
    centered_rows = values - jnp.mean(values, axis=-1, keepdims=True)
    inverse_deviation = lax.rsqrt(
        jnp.mean(centered_rows * centered_rows, axis=-1, keepdims=True) + 1e-05
    )
    standardized_input = centered_rows * inverse_deviation
    normalized_rows = (standardized_input * gain_weight + shift_bias).astype(jnp.bfloat16)
    return (normalized_rows, standardized_input, inverse_deviation)


def layer_norm_backward(normed_gradient, standardized_input, inverse_deviation, gain_weight):
    incoming_gradient = normed_gradient * gain_weight
    gradient_mean = jnp.mean(incoming_gradient, axis=-1, keepdims=True)
    cross_term_mean = jnp.mean(incoming_gradient * standardized_input, axis=-1, keepdims=True)
    return inverse_deviation * (
        incoming_gradient - gradient_mean - standardized_input * cross_term_mean
    )


def attend_grad(qkv, out_grad, lengths):
    count = qkv.shape[0]
    width = out_grad.shape[1]
    heads = width // HEAD
    scale = float(HEAD) ** (-0.5)
    bounds = jnp.cumsum(lengths)
    places = jnp.arange(count, dtype=jnp.int32)
    segment = jnp.sum((places[:, None] >= bounds[None, :]).astype(jnp.int32), axis=1)
    same = segment[:, None] == segment[None, :]
    contract_last = (((1,), (1,)), ((), ()))
    contract_first = (((0,), (0,)), ((), ()))

    def one_head(head, grads):
        query = lax.dynamic_slice_in_dim(qkv, head * HEAD, HEAD, 1)
        key_part = lax.dynamic_slice_in_dim(qkv, width + head * HEAD, HEAD, 1)
        value = lax.dynamic_slice_in_dim(qkv, 2 * width + head * HEAD, HEAD, 1)
        dout = lax.dynamic_slice_in_dim(out_grad, head * HEAD, HEAD, 1)
        scores = (
            lax.dot_general(query, key_part, contract_last, preferred_element_type=jnp.float32)
            * scale
        )
        scores = jnp.where(same, scores, -1e30)
        top = jnp.max(scores, axis=-1, keepdims=True)
        expo = jnp.exp(scores - top)
        probs = expo / jnp.sum(expo, axis=-1, keepdims=True)
        weights = probs.astype(jnp.bfloat16)
        dprob = lax.dot_general(dout, value, contract_last, preferred_element_type=jnp.float32)
        inner = jnp.sum(dprob * probs, axis=-1, keepdims=True)
        dscore = (scale * probs * (dprob - inner)).astype(jnp.bfloat16)
        dquery = jnp.dot(dscore, key_part, preferred_element_type=jnp.float32).astype(jnp.bfloat16)
        dkey = lax.dot_general(
            dscore, query, contract_first, preferred_element_type=jnp.float32
        ).astype(jnp.bfloat16)
        dvalue = lax.dot_general(
            weights, dout, contract_first, preferred_element_type=jnp.float32
        ).astype(jnp.bfloat16)
        grads = lax.dynamic_update_slice_in_dim(grads, dquery, head * HEAD, 1)
        grads = lax.dynamic_update_slice_in_dim(grads, dkey, width + head * HEAD, 1)
        grads = lax.dynamic_update_slice_in_dim(grads, dvalue, 2 * width + head * HEAD, 1)
        return grads

    empty = jnp.zeros((count, 3 * width), jnp.bfloat16)
    return lax.fori_loop(0, heads, one_head, empty)


def per_device(
    block_input,
    upstream,
    w_qkv,
    w_out,
    layer_norm_gain,
    layer_norm_bias,
    send_order,
    recv_order,
    patch_lengths,
):
    inputs = block_input[0]
    upper = upstream[0]
    projection = w_qkv[0]
    gain_weight = layer_norm_gain[0]
    shift_bias = layer_norm_bias[0]
    sending = send_order[0, 0]
    placing = recv_order[0, 0]
    lengths = patch_lengths[0, 0]
    undo_send = jnp.argsort(sending)
    undo_place = jnp.argsort(placing)
    contract_last = (((1,), (1,)), ((), ()))
    out_common = lax.dot_general(
        upper, w_out[0], contract_last, preferred_element_type=jnp.float32
    ).astype(jnp.bfloat16)
    out_sent = out_common[sending]
    patch_token_rows = lax.all_to_all(
        inputs[sending], "seq", split_axis=0, concat_axis=0, tiled=True
    )[placing]
    normalized_rows, standardized_input, inverse_deviation = layer_normalize(
        patch_token_rows, gain_weight, shift_bias
    )
    qkv = jnp.dot(normalized_rows, projection, preferred_element_type=jnp.float32).astype(
        jnp.bfloat16
    )
    out_grad = lax.all_to_all(out_sent, "seq", split_axis=0, concat_axis=0, tiled=True)[placing]
    dqkv = attend_grad(qkv, out_grad, lengths)
    normed_gradient = lax.dot_general(
        dqkv, projection, contract_last, preferred_element_type=jnp.float32
    )
    patch_attention_branch = layer_norm_backward(
        normed_gradient, standardized_input, inverse_deviation, gain_weight
    ).astype(jnp.bfloat16)
    branch_output = lax.all_to_all(
        patch_attention_branch[undo_place], "seq", split_axis=0, concat_axis=0, tiled=True
    )[undo_send]
    total = (upper.astype(jnp.float32) + branch_output.astype(jnp.float32)).astype(jnp.bfloat16)
    handed = from_behind(total, "section", -1)
    return handed[None]


def solution(mesh):
    return jax.shard_map(
        per_device,
        mesh=mesh,
        in_specs=(
            P("section", "seq", None),
            P("section", "seq", None),
            P("section", None, None),
            P("section", None, None),
            P("section", None),
            P("section", None),
            P("section", "seq", None),
            P("section", "seq", None),
            P("section", "seq", None),
        ),
        out_specs=P("section", "seq", None),
        check_vma=False,
    )
```

profile of v0, /device:TPU:1, one launch (start us, length us, event | category | flops | bytes accessed | tf_op | source)
XLA Modules:
  0.0 81.0 jit_solution(156622973408188727)
XLA Ops:
  0.0 0.8 compare_select_fusion.1
  0.8 1.3 %convolution_convert_fusion.4 = bf16[256,256]{1,0:T(8,128)(2,1)S(1)} fusion(bf16[1,256,512]{2,1,0:T(8,128)(2,1)} %param.14, bf16[1,256,512]{2,1,0:T(8,128)(2,1)} %param.12), kind=kOutput, calls=%fused_computation.36 | convolution fusion | flops 67174400 | bytes 655360 | tf_op jit(solution)/shard_map/dot_general | solution.py:102
  2.1 1.8 %gather_fusion.2 = bf16[256,256]{1,0:T(8,128)(2,1)} fusion(bf16[256,256]{1,0:T(8,128)(2,1)S(1)} %convolution_convert_fusion.4, s32[1024]{0:T(1024)S(1)} %pad_clamp_fusion.3), kind=kCustom, calls=%fused_computation.2 | custom fusion | bytes 263168 | tf_op jit(solution)/shard_map/gather | solution.py:105
  3.8 6.5 %all-to-all-start.1 = ((bf16[8,32,256]{2,1,0:T(8,128)(2,1)}), bf16[8,32,256]{2,1,0:T(8,128)(2,1)S(1)}, u32[]{:S(2)}, u32[]{:S(2)}) async-start(bf16[8,32,256]{2,1,0:T(8,128)(2,1)} %bitcast.12), calls=%async_computation.1 | async-start | bytes 262144 | tf_op jit(solution)/shard_map/all_to_all | solution.py:115
  10.4 1.9 %gather_fusion = bf16[256,512]{1,0:T(8,128)(2,1)} fusion(bf16[256,512]{1,0:T(8,128)(2,1)S(1)} %bitcast.43, s32[1024]{0:T(1024)S(1)} %pad_clamp_fusion.3), kind=kCustom, calls=%fused_computation | custom fusion | bytes 525312 | tf_op jit(solution)/shard_map/gather | solution.py:107
  12.2 4.3 %all-to-all-done.1 = bf16[8,32,256]{2,1,0:T(8,128)(2,1)S(1)} async-done(((bf16[8,32,256]{2,1,0:T(8,128)(2,1)}), bf16[8,32,256]{2,1,0:T(8,128)(2,1)S(1)}, u32[]{:S(2)}, u32[]{:S(2)}) %all-to-all-start.1) | async-done | bytes 131104 | tf_op jit(solution)/shard_map/all_to_all | solution.py:115
  16.6 3.4 %all-to-all-start = ((bf16[8,32,512]{2,1,0:T(8,128)(2,1)}), bf16[8,32,512]{2,1,0:T(8,128)(2,1)S(1)}, u32[]{:S(2)}, u32[]{:S(2)}) async-start(bf16[8,32,512]{2,1,0:T(8,128)(2,1)} %bitcast.4), calls=%async_computation | async-start | bytes 524288 | tf_op jit(solution)/shard_map/all_to_all | solution.py:106
  20.0 0.6 copy-done.7
  20.9 3.2 %sort.31 = (s32[256]{0:T(256)}, s32[256]{0:T(256)S(1)}) sort(s32[256]{0:T(256)S(1)} %bitcast.48, s32[256]{0:T(256)S(1)} %iota.11), dimensions={0}, to_apply=%region_11.12 | sort | flops 2048 | bytes 4096 | tf_op jit(solution)/shard_map/jit(argsort)/sort | solution.py:100
  24.1 1.1 %gather_fusion.3 = bf16[256,256]{1,0:T(8,128)(2,1)S(1)} fusion(bf16[256,256]{1,0:T(8,128)(2,1)S(1)} %bitcast.44, s32[1024]{0:T(1024)S(1)} %pad_clamp_fusion.2), kind=kCustom, calls=%fused_computation.3 | custom fusion | bytes 263168 | tf_op jit(solution)/shard_map/gather | solution.py:115
  25.3 1.8 %all-to-all-done = bf16[8,32,512]{2,1,0:T(8,128)(2,1)S(1)} async-done(((bf16[8,32,512]{2,1,0:T(8,128)(2,1)}), bf16[8,32,512]{2,1,0:T(8,128)(2,1)S(1)}, u32[]{:S(2)}, u32[]{:S(2)}) %all-to-all-start) | async-done | bytes 262176 | tf_op jit(solution)/shard_map/all_to_all | solution.py:106
  27.1 1.2 %gather_fusion.1 = bf16[256,512]{1,0:T(8,128)(2,1)S(1)} fusion(bf16[256,512]{1,0:T(8,128)(2,1)S(1)} %bitcast.41, s32[1024]{0:T(1024)S(1)} %pad_clamp_fusion.2), kind=kCustom, calls=%fused_computation.1 | custom fusion | bytes 525312 | tf_op jit(solution)/shard_map/gather | solution.py:106
  29.3 0.4 convolution_convert_fusion.3
  29.7 24.9 %while.16 = (s32[]{:T(128)}, bf16[256,768]{0,1:T(8,128)(2,1)S(1)}, bf16[256,768]{1,0:T(8,128)(2,1)S(1)}, bf16[256,256]{1,0:T(8,128)(2,1)S(1)}, s32[256]{0:T(256)...) while((s32[]{:T(128)}, bf16[256,768]{0,1:T(8,128)(2,1)S(1)}, ...), condition=%wide.region_8.9_spmd.clone, body=%wide.region_4.0_spmd.clone.sunk | while | flops 11742479 | bytes 2725180 | solution.py:77
  54.6 0.6 fusion.45
  55.4 1.9 %gather_fusion.4 = bf16[256,512]{1,0:T(8,128)(2,1)} fusion(bf16[256,512]{1,0:T(8,128)(2,1)S(1)} %fusion.35, s32[1024]{0:T(1024)S(1)} %pad_clamp_fusion.1), kind=kCustom, calls=%fused_computation.4 | custom fusion | bytes 525312 | tf_op jit(solution)/shard_map/gather | solution.py:124
  57.3 3.9 %all-to-all-start.2 = ((bf16[8,32,512]{2,1,0:T(8,128)(2,1)}), bf16[8,32,512]{2,1,0:T(8,128)(2,1)S(1)}, u32[]{:S(2)}, u32[]{:S(2)}) async-start(bf16[8,32,512]{2,1,0:T(8,128)(2,1)} %bitcast.17), calls=%async_computation.2 | async-start | bytes 524288 | tf_op jit(solution)/shard_map/all_to_all | solution.py:123
  61.1 0.7 copy-done.4
  61.8 3.2 %sort.32 = (s32[256]{0:T(256)}, s32[256]{0:T(256)S(1)}) sort(s32[256]{0:T(256)S(1)} %bitcast.49, s32[256]{0:T(256)S(1)} %iota.12), dimensions={0}, to_apply=%region_12.13 | sort | flops 2048 | bytes 4096 | tf_op jit(solution)/shard_map/jit(argsort)/sort | solution.py:99
  65.0 3.3 %all-to-all-done.2 = bf16[8,32,512]{2,1,0:T(8,128)(2,1)S(1)} async-done(((bf16[8,32,512]{2,1,0:T(8,128)(2,1)}), bf16[8,32,512]{2,1,0:T(8,128)(2,1)S(1)}, u32[]{:S(2)}, u32[]{:S(2)}) %all-to-all-start.2) | async-done | bytes 262176 | tf_op jit(solution)/shard_map/all_to_all | solution.py:123
  68.3 1.2 %gather_fusion.5 = bf16[256,512]{1,0:T(8,128)(2,1)S(1)} fusion(bf16[256,512]{1,0:T(8,128)(2,1)S(1)} %bitcast.42, s32[1024]{0:T(1024)S(1)} %pad_clamp_fusion), kind=kCustom, calls=%fused_computation.5 | custom fusion | bytes 525312 | tf_op jit(solution)/shard_map/gather | solution.py:123
  69.5 5.6 %collective-permute-start = (bf16[256,512]{1,0:T(8,128)(2,1)S(1)}, bf16[256,512]{1,0:T(8,128)(2,1)S(1)}, u32[]{:S(2)}, u32[]{:S(2)}) collective-permute-start(bf16[256,512]{1,0:T(8,128)(2,1)S(1)} %add_convert_fusion), channel_id=1, source_target_pairs={{1,0},{2,1},{3,2},{5,4},{6,5},{7,6},{9,8},{10,9},{11,10},{13,12},{... | collective-permute-start | bytes 786440 | tf_op jit(solution)/shard_map/ppermute | solution.py:12
  75.2 5.1 %collective-permute-done = bf16[256,512]{1,0:T(8,128)(2,1)S(1)} collective-permute-done((bf16[256,512]{1,0:T(8,128)(2,1)S(1)}, bf16[256,512]{1,0:T(8,128)(2,1)S(1)}, u32[]{:S(2)}, u32[]{:S(2)}) %collective-permute-start) | collective-permute-done | bytes 262176 | tf_op jit(solution)/shard_map/ppermute | solution.py:12
  80.3 0.7 copy.20
  (145 shorter events, 26.2 us)
Async XLA Ops:
  0.0 28.6 %copy-start = (bf16[1,512,768]{2,1,0:T(8,128)(2,1)S(1)}, bf16[1,512,768]{2,1,0:T(8,128)(2,1)}, u32[]{:S(2)}) copy-start(bf16[1,512,768]{2,1,0:T(8,128)(2,1)} %param.13) | copy-start | bytes 2359300
  3.8 6.5 %copy-start.1 = (bf16[1,256,512]{2,1,0:T(8,128)(2,1)S(1)}, bf16[1,256,512]{2,1,0:T(8,128)(2,1)}, u32[]{:S(2)}) copy-start(bf16[1,256,512]{2,1,0:T(8,128)(2,1)} %param.11) | copy-start | bytes 786436
  3.8 12.7 %all-to-all-start.1 = ((bf16[8,32,256]{2,1,0:T(8,128)(2,1)}), bf16[8,32,256]{2,1,0:T(8,128)(2,1)S(1)}, u32[]{:S(2)}, u32[]{:S(2)}) async-start(bf16[8,32,256]{2,1,0:T(8,128)(2,1)} %bitcast.12), calls=%async_computation.1 | async-start | bytes 262144 | tf_op jit(solution)/shard_map/all_to_all | solution.py:115
  10.4 1.9 %copy-start.3 = (s32[1,1,256]{2,1,0:T(1,128)S(1)}, s32[1,1,256]{2,1,0:T(1,128)}, u32[]{:S(2)}) copy-start(s32[1,1,256]{2,1,0:T(1,128)} %param.18) | copy-start | bytes 3076
  16.6 10.5 %all-to-all-start = ((bf16[8,32,512]{2,1,0:T(8,128)(2,1)}), bf16[8,32,512]{2,1,0:T(8,128)(2,1)S(1)}, u32[]{:S(2)}, u32[]{:S(2)}) async-start(bf16[8,32,512]{2,1,0:T(8,128)(2,1)} %bitcast.4), calls=%async_computation | async-start | bytes 524288 | tf_op jit(solution)/shard_map/all_to_all | solution.py:106
  20.0 0.7 copy-start.7
  28.3 0.7 copy-start.6
  28.6 0.7 copy-start.5
  57.3 11.1 %all-to-all-start.2 = ((bf16[8,32,512]{2,1,0:T(8,128)(2,1)}), bf16[8,32,512]{2,1,0:T(8,128)(2,1)S(1)}, u32[]{:S(2)}, u32[]{:S(2)}) async-start(bf16[8,32,512]{2,1,0:T(8,128)(2,1)} %bitcast.17), calls=%async_computation.2 | async-start | bytes 524288 | tf_op jit(solution)/shard_map/all_to_all | solution.py:123
  61.1 0.7 copy-start.4
  68.3 1.2 %copy-start.2 = (bf16[1,256,512]{2,1,0:T(8,128)(2,1)S(1)}, bf16[1,256,512]{2,1,0:T(8,128)(2,1)}, u32[]{:S(2)}) copy-start(bf16[1,256,512]{2,1,0:T(8,128)(2,1)} %param.12) | copy-start | bytes 786436
  69.5 10.8 %collective-permute-start = (bf16[256,512]{1,0:T(8,128)(2,1)S(1)}, bf16[256,512]{1,0:T(8,128)(2,1)S(1)}, u32[]{:S(2)}, u32[]{:S(2)}) collective-permute-start(bf16[256,512]{1,0:T(8,128)(2,1)S(1)} %add_convert_fusion), channel_id=1, source_target_pairs={{1,0},{2,1},{3,2},{5,4},{6,5},{7,6},{9,8},{10,9},{11,10},{13,12},{... | collective-permute-start | bytes 786440 | tf_op jit(solution)/shard_map/ppermute | solution.py:12
where the time goes:
time: 81.5 us; the launch traced here: 81 us
  matrix products  24.5 us (30%)
  starting transfers between devices  19.4 us (24%)
  waiting for transfers between devices  14.5 us (18%)
  local copies, waits for them, and re-layouts  11.7 us (14%)
  other arithmetic  10.4 us (13%)
    all_to_all x1, starting transfers between devices, per_device(): lax.all_to_all(out_sent, 'seq', split_axis=0, concat_axis=0, tiled=True)  6.52 us
    ppermute x1, starting transfers between devices, from_behind(): return lax.ppermute(array, axis, pairs)  5.62 us
    ppermute x1, waiting for transfers between devices, from_behind(): return lax.ppermute(array, axis, pairs)  5.13 us
    dot_general x16, matrix products, one_head(): lax.dot_general(query, key_part, contract_last, preferred_element_type=jn...  5.1 us
    dot_general x16, matrix products, one_head(): lax.dot_general(dout, value, contract_last, preferred_element_type=jnp.fl...  4.81 us
    all_to_all x1, waiting for transfers between devices, per_device(): lax.all_to_all(out_sent, 'seq', split_axis=0, concat_axis=0, tiled=True)  4.33 us
    dot_general x16, matrix products, one_head(): lax.dot_general(weights, dout, contract_first, preferred_element_type=jnp...  4.22 us
    dot_general x16, matrix products, one_head(): lax.dot_general(dscore, query, contract_first, preferred_element_type=jnp...  4.16 us
  transfers between devices with their start and end apart: 4, of which 4 were waited for; matrix products, arithmetic and copies ran while one was open for 12% of the time, Pallas kernels for 0%

commit v1 on v0

v1 whole, which is shorter than its diff:
```python
import functools
import math

import jax
import jax.numpy as jnp
from jax import lax
from jax.experimental import pallas as pl
from jax.experimental.pallas import tpu as pltpu
from jax.sharding import PartitionSpec as P

HEAD = 16
MESH = pl.DeviceIdType.MESH
LAST = (((1,), (1,)), ((), ()))
GROUP = 4


def dot(a, b):
    return jnp.dot(a, b, preferred_element_type=jnp.float32)


def dot_nt(a, b):
    return lax.dot_general(a, b, LAST, preferred_element_type=jnp.float32)


def each(first, count, body):
    if count - first <= 8:
        for step in range(first, count):
            body(step)
    else:
        lax.fori_loop(first, count, lambda step, carry: (body(step), carry)[1], 0)


def iota(shape, axis):
    return lax.broadcasted_iota(jnp.int32, shape, axis)


def kernel(
    n,
    sections,
    x_ref,
    up_ref,
    w_ref,
    wo_ref,
    gain_ref,
    bias_ref,
    send_ref,
    recv_ref,
    len_ref,
    out_ref,
    send_x,
    recv_x,
    send_o,
    recv_o,
    send_b,
    recv_b,
    up_next,
    order_own,
    order_next,
    xhat_ref,
    q_ref,
    k_ref,
    v_ref,
    kt_ref,
    do_ref,
    feat_q,
    feat_k,
    dqt_ref,
    dk_ref,
    dv_ref,
    sx_sem,
    rx_sem,
    so_sem,
    ro_sem,
    sb_sem,
    rb_sem,
    up_sem,
    order_sem,
):
    me = lax.axis_index("seq")
    section = lax.axis_index("section")
    rows, wide = x_ref.shape[1], x_ref.shape[2]
    width = wo_ref.shape[1]
    slot = send_x.shape[1]
    block = rows // n
    half = 128

    def spread(values):
        if slot == block:
            return values.reshape(n, slot, values.shape[1])
        place = iota((n * slot, rows), 0)
        source = jnp.where(place % slot < block, place // slot * block + place % slot, -1)
        pick = (source == iota((n * slot, rows), 1)).astype(jnp.bfloat16)
        return dot(pick, values).astype(jnp.bfloat16).reshape(n, slot, values.shape[1])

    def gather(values):
        values = values.reshape(n * slot, values.shape[2])
        if slot == block:
            return values
        place = iota((rows, n * slot), 0)
        pick = (place // block * slot + place % block == iota((rows, n * slot), 1)).astype(jnp.bfloat16)
        return dot(pick, values).astype(jnp.bfloat16)

    def x_copy(local, there, peer):
        return pltpu.make_async_remote_copy(
            send_x.at[local], recv_x.at[there], sx_sem.at[local], rx_sem.at[there],
            device_id=(peer, section), device_id_type=MESH,
        )

    def o_copy(local, there, peer):
        return pltpu.make_async_remote_copy(
            send_o.at[local], recv_o.at[there], so_sem.at[local], ro_sem.at[there],
            device_id=(peer, section), device_id_type=MESH,
        )

    def b_copy(local, there, peer):
        return pltpu.make_async_remote_copy(
            send_b.at[local], recv_b.at[there], sb_sem.at[local], rb_sem.at[there],
            device_id=(peer, section - 1), device_id_type=MESH,
        )

    def up_copy():
        return pltpu.make_async_remote_copy(
            up_ref.at[0], up_next, up_sem.at[0], up_sem.at[1],
            device_id=(me, section - 1), device_id_type=MESH,
        )

    def order_copy():
        return pltpu.make_async_remote_copy(
            order_own, order_next, order_sem.at[0], order_sem.at[1],
            device_id=(me, section - 1), device_id_type=MESH,
        )

    barrier = pltpu.get_barrier_semaphore()

    @pl.when(section > 0)
    def _():
        def greet(step):
            pl.semaphore_signal(
                barrier, inc=1, device_id=(lax.rem(me + step, n), section), device_id_type=MESH
            )

        each(1, n, greet)

    @pl.when(section < sections - 1)
    def _():
        def greet(step):
            pl.semaphore_signal(
                barrier, inc=1, device_id=(lax.rem(me + step, n), section + 1), device_id_type=MESH
            )

        each(0, n, greet)

    @pl.when(section > 0)
    def _():
        order_own[...] = jnp.broadcast_to(send_ref[0], order_own.shape)
        row_of = send_ref[0].astype(jnp.float32)
        eye = iota((rows, rows), 0) == iota((rows, rows), 1)
        column = jnp.sum(jnp.where(eye, row_of, 0.0), axis=1, keepdims=True).astype(jnp.int32)
        pick = jnp.where(column == iota((rows, rows), 1), 1.0, 0.0).astype(jnp.bfloat16)
        send_x[...] = spread(dot(pick, x_ref[0]).astype(jnp.bfloat16))
        pl.semaphore_wait(barrier, 2 * n - 1)
        each(1, n, lambda step: x_copy(lax.rem(me + step, n), me, lax.rem(me + step, n)).start())
        out_common = dot_nt(up_ref[0], wo_ref[0]).astype(jnp.bfloat16)
        send_o[...] = spread(dot(pick, out_common).astype(jnp.bfloat16))
        each(1, n, lambda step: o_copy(lax.rem(me + step, n), me, lax.rem(me + step, n)).start())
        up_copy().start()
        order_copy().start()
        recv_x[me] = send_x[me]
        recv_o[me] = send_o[me]

        place = iota((1, rows), 1)
        end = jnp.int32(0)
        segment = jnp.zeros((1, rows), jnp.float32)
        for patch in range(len_ref.shape[2]):
            end = end + len_ref[0, 0, patch]
            segment = segment + jnp.where(place >= end, 1.0, 0.0)
        at = recv_ref[0] == iota((rows, rows), 0)
        patch_of = jnp.sum(jnp.where(at, segment, 0.0), axis=1, keepdims=True).astype(jnp.int32)
        lanes = iota((rows, half), 1)
        feat_k[...] = jnp.where(patch_of == lanes, 1.0, 0.0).astype(jnp.bfloat16)
        feat_q[...] = jnp.where(patch_of == lanes, 0.0, -1e30).astype(jnp.bfloat16)

        def x_wait(step):
            peer = lax.rem(me + step, n)
            x_copy(peer, peer, peer).wait_recv()

        each(1, n, x_wait)
        values = gather(recv_x[...]).astype(jnp.float32)
        centered = values - jnp.mean(values, axis=-1, keepdims=True)
        inverse = lax.rsqrt(jnp.mean(centered * centered, axis=-1, keepdims=True) + 1e-05)
        xhat = centered * inverse
        xhat_ref[...] = xhat
        normed = (xhat * gain_ref[...] + bias_ref[...]).astype(jnp.bfloat16)
        q_ref[...] = dot(normed, w_ref[0, :, :width]).astype(jnp.bfloat16)
        key = dot(normed, w_ref[0, :, width : 2 * width]).astype(jnp.bfloat16)
        k_ref[...] = key
        kt_ref[...] = key.astype(jnp.float32).T.astype(jnp.bfloat16)
        v_ref[...] = dot(normed, w_ref[0, :, 2 * width :]).astype(jnp.bfloat16)

        def o_wait(step):
            peer = lax.rem(me + step, n)
            o_copy(peer, peer, peer).wait_recv()

        each(1, n, o_wait)
        do_ref[...] = gather(recv_o[...])

        rate = float(HEAD) ** (-0.5) * math.log2(math.e)
        lane_head = iota((rows, half), 1) // HEAD
        zero = jnp.zeros((rows, half), jnp.bfloat16)
        for part in range(width // half):
            columns = slice(part * half, (part + 1) * half)

            def some_heads(group, carry, columns=columns, part=part):
                query, key, value, dout = q_ref[:, columns], k_ref[:, columns], v_ref[:, columns], do_ref[:, columns]
                query_right = jnp.concatenate([query, feat_q[...]], axis=1)
                mine = [lane_head == group * GROUP + i for i in range(GROUP)]
                keys = jnp.concatenate(
                    [jnp.concatenate([jnp.where(m, key, zero), feat_k[...]], axis=1) for m in mine], axis=0
                )
                values = jnp.concatenate([jnp.where(m, value, zero) for m in mine], axis=0)
                scores = dot_nt(keys, query_right)
                dprobs = dot_nt(values, dout)
                weights, dscores = [], []
                for i in range(GROUP):
                    score = scores[i * rows : (i + 1) * rows]
                    dprob = dprobs[i * rows : (i + 1) * rows]
                    expo = jnp.exp2((score - jnp.max(score, axis=0, keepdims=True)) * rate)
                    probs = expo * (1.0 / jnp.sum(expo, axis=0, keepdims=True))
                    inner = jnp.sum(dprob * probs, axis=0, keepdims=True)
                    weights.append(probs.astype(jnp.bfloat16))
                    dscores.append((probs * (dprob - inner)).astype(jnp.bfloat16))
                dkeys = dot(jnp.concatenate(dscores, axis=0), query)
                dvalues = dot(jnp.concatenate(weights, axis=0), dout)
                dkey, dvalue = dk_ref[:, columns], dv_ref[:, columns]
                for i in range(GROUP):
                    dkey = jnp.where(mine[i], dkeys[i * rows : (i + 1) * rows], dkey)
                    dvalue = jnp.where(mine[i], dvalues[i * rows : (i + 1) * rows], dvalue)
                    start = pl.multiple_of(part * half + (group * GROUP + i) * HEAD, HEAD)
                    dqt_ref[pl.ds(start, HEAD), :] = dot(kt_ref[pl.ds(start, HEAD), :], dscores[i])
                dk_ref[:, columns] = dkey
                dv_ref[:, columns] = dvalue
                return carry

            lax.fori_loop(0, half // HEAD // GROUP, some_heads, 0)

        scale = float(HEAD) ** (-0.5)
        dquery = (dqt_ref[...].T * scale).astype(jnp.bfloat16)
        dkey = (dk_ref[...] * scale).astype(jnp.bfloat16)
        dqkv = jnp.concatenate([dquery, dkey, dv_ref[...].astype(jnp.bfloat16)], axis=1)
        grad = dot_nt(dqkv, w_ref[0]) * gain_ref[...]
        xhat = xhat_ref[...]
        mean = jnp.mean(grad, axis=-1, keepdims=True)
        cross = jnp.mean(grad * xhat, axis=-1, keepdims=True)
        branch = inverse * (grad - mean - xhat * cross)
        send_b[...] = spread(branch.astype(jnp.bfloat16))
        each(0, n, lambda step: b_copy(lax.rem(me + step, n), me, lax.rem(me + step, n)).start())

    @pl.when(section < sections - 1)
    def _():
        order_copy().wait_recv()
        up_copy().wait_recv()
        pick = jnp.where(order_next[0:1, :] == iota((rows, rows), 0), 1.0, 0.0).astype(jnp.bfloat16)

        def b_wait(step):
            peer = lax.rem(me + step, n)
            b_copy(peer, peer, peer).wait_recv()

        each(0, n, b_wait)
        branch = dot(pick, gather(recv_b[...]))
        out_ref[0] = (up_next[...].astype(jnp.float32) + branch).astype(jnp.bfloat16)

    @pl.when(section == sections - 1)
    def _():
        out_ref[...] = jnp.zeros_like(out_ref)

    @pl.when(section > 0)
    def _():
        def sent(step):
            peer = lax.rem(me + step, n)
            x_copy(peer, me, peer).wait_send()
            o_copy(peer, me, peer).wait_send()

        each(1, n, sent)

        def sent_back(step):
            peer = lax.rem(me + step, n)
            b_copy(peer, me, peer).wait_send()

        each(0, n, sent_back)
        up_copy().wait_send()
        order_copy().wait_send()


def per_device(x, up, w_qkv, w_out, gain, bias, send_order, recv_order, lengths):
    n, sections = lax.axis_size("seq"), lax.axis_size("section")
    rows, wide = x.shape[1], x.shape[2]
    width = w_out.shape[1]
    slot = max(rows // n, 16)
    vmem = pl.BlockSpec(memory_space=pltpu.VMEM)
    smem = pl.BlockSpec(memory_space=pltpu.SMEM)
    bf16, f32 = jnp.bfloat16, jnp.float32
    dma = pltpu.SemaphoreType.DMA
    return pl.pallas_call(
        functools.partial(kernel, n, sections),
        out_shape=jax.ShapeDtypeStruct(x.shape, bf16),
        in_specs=[vmem] * 8 + [smem],
        out_specs=vmem,
        scratch_shapes=[
            pltpu.VMEM((n, slot, wide), bf16),
            pltpu.VMEM((n, slot, wide), bf16),
            pltpu.VMEM((n, slot, width), bf16),
            pltpu.VMEM((n, slot, width), bf16),
            pltpu.VMEM((n, slot, wide), bf16),
            pltpu.VMEM((n, slot, wide), bf16),
            pltpu.VMEM((rows, wide), bf16),
            pltpu.VMEM((8, rows), jnp.int32),
            pltpu.VMEM((8, rows), jnp.int32),
            pltpu.VMEM((rows, wide), f32),
            pltpu.VMEM((rows, width), bf16),
            pltpu.VMEM((rows, width), bf16),
            pltpu.VMEM((rows, width), bf16),
            pltpu.VMEM((width, rows), bf16),
            pltpu.VMEM((rows, width), bf16),
            pltpu.VMEM((rows, 128), bf16),
            pltpu.VMEM((rows, 128), bf16),
            pltpu.VMEM((width, rows), f32),
            pltpu.VMEM((rows, width), f32),
            pltpu.VMEM((rows, width), f32),
            dma((n,)),
            dma((n,)),
            dma((n,)),
            dma((n,)),
            dma((n,)),
            dma((n,)),
            dma((2,)),
            dma((2,)),
        ],
        compiler_params=pltpu.CompilerParams(
            collective_id=0, has_side_effects=True, vmem_limit_bytes=40 * 1024 * 1024
        ),
        name="patch_attention_grad",
    )(x, up, w_qkv, w_out, gain, bias, send_order, recv_order, lengths)


def solution(mesh):
    return jax.shard_map(
        per_device,
        mesh=mesh,
        in_specs=(
            P("section", "seq", None),
            P("section", "seq", None),
            P("section", None, None),
            P("section", None, None),
            P("section", None),
            P("section", None),
            P("section", "seq", None),
            P("section", "seq", None),
            P("section", "seq", None),
        ),
        out_specs=P("section", "seq", None),
        check_vma=False,
    )
```

time: 81.5 us -> 36.5 us (0.45)
  Pallas kernels: 0 us -> 28.1 us
  matrix products: 24.5 us -> 0 us
  starting transfers between devices: 19.4 us -> 0 us
  waiting for transfers between devices: 14.5 us -> 0 us
  other arithmetic: 10.4 us -> 0 us
  local copies, waits for them, and re-layouts: 11.7 us -> 8.06 us
    pallas_call x0 -> x1, Pallas kernels: none -> 28.1 us  [per_device(): pl.pallas_call(functools.partial(kernel, n, sections), out_shape=jax.Shap...]
    dot_general x83 -> x0, matrix products: 24.5 us -> none  [the longest x16 5.1 us: one_head(): lax.dot_general(query, key_part, contract_last, preferred_element_type=jn...]
    all_to_all x3 -> x0, starting transfers between devices: 13.8 us -> none  [the longest x1 6.52 us: per_device(): lax.all_to_all(out_sent, 'seq', split_axis=0, concat_axis=0, tiled=True)]
    all_to_all x3 -> x0, waiting for transfers between devices: 9.38 us -> none  [the longest x1 4.33 us: per_device(): lax.all_to_all(out_sent, 'seq', split_axis=0, concat_axis=0, tiled=True)]
    gather x6 -> x0, local copies, waits for them, and re-layouts: 8.95 us -> none  [the longest x1 1.85 us: per_device(): inputs[sending]]
    sort x2 -> x0, other arithmetic: 6.39 us -> none  [the longest x1 3.2 us: per_device(): undo_place = jnp.argsort(placing)]
    ppermute x1 -> x0, starting transfers between devices: 5.62 us -> none  [from_behind(): return lax.ppermute(array, axis, pairs)]
    unnamed x17 -> x19, local copies, waits for them, and re-layouts: 2.72 us -> 8.06 us
  transfers between devices with their start and end apart: 4 -> 0, of which waited for: 4 -> 0; matrix products, arithmetic and copies ran while one was open for 12% -> 0% of each run, Pallas kernels for 0% -> 0%
where the time goes in v1:
time: 36.5 us; the launch traced here: 36.1 us
  Pallas kernels  28.1 us (77%)
  local copies, waits for them, and re-layouts  8.06 us (22%)
    pallas_call x1, Pallas kernels, per_device(): pl.pallas_call(functools.partial(kernel, n, sections), out_shape=jax.Shap...  28.1 us
    unnamed x19, local copies, waits for them, and re-layouts  8.06 us

profile of v1, /device:TPU:1, one launch (start us, length us, event | category | flops | bytes accessed | tf_op | source)
XLA Modules:
  0.0 36.1 jit_solution(3163586079328372639)
XLA Ops:
  0.0 0.0 copy-start
  0.0 1.1 %copy-done = bf16[1,512,768]{2,1,0:T(8,128)(2,1)S(1)} copy-done((bf16[1,512,768]{2,1,0:T(8,128)(2,1)S(1)}, bf16[1,512,768]{2,1,0:T(8,128)(2,1)}, u32[]{:S(2)}) %copy-start) | copy-done | bytes 786456
  1.1 0.0 copy-start.1
  1.1 0.9 %copy-done.1 = bf16[1,256,512]{2,1,0:T(8,128)(2,1)S(1)} copy-done((bf16[1,256,512]{2,1,0:T(8,128)(2,1)S(1)}, bf16[1,256,512]{2,1,0:T(8,128)(2,1)}, u32[]{:S(2)}) %copy-start.1) | copy-done | bytes 262168
  2.1 0.0 copy-start.2
  2.1 0.9 %copy-done.2 = bf16[1,256,512]{2,1,0:T(8,128)(2,1)S(1)} copy-done((bf16[1,256,512]{2,1,0:T(8,128)(2,1)S(1)}, bf16[1,256,512]{2,1,0:T(8,128)(2,1)}, u32[]{:S(2)}) %copy-start.2) | copy-done | bytes 262168
  3.0 0.0 copy-start.3
  3.0 0.9 %copy-done.3 = bf16[1,256,512]{2,1,0:T(8,128)(2,1)S(1)} copy-done((bf16[1,256,512]{2,1,0:T(8,128)(2,1)S(1)}, bf16[1,256,512]{2,1,0:T(8,128)(2,1)}, u32[]{:S(2)}) %copy-start.3) | copy-done | bytes 262168
  4.0 0.0 copy-start.4
  4.0 0.7 %copy-done.4 = f32[1,512]{1,0:T(1,128)S(1)} copy-done((f32[1,512]{1,0:T(1,128)S(1)}, f32[1,512]{1,0:T(1,128)}, u32[]{:S(2)}) %copy-start.4) | copy-done | bytes 2072
  4.7 0.0 copy-start.5
  4.7 0.7 %copy-done.5 = f32[1,512]{1,0:T(1,128)S(1)} copy-done((f32[1,512]{1,0:T(1,128)S(1)}, f32[1,512]{1,0:T(1,128)}, u32[]{:S(2)}) %copy-start.5) | copy-done | bytes 2072
  5.3 0.0 copy-start.6
  5.4 0.7 %copy-done.6 = s32[1,1,256]{2,1,0:T(1,128)S(1)} copy-done((s32[1,1,256]{2,1,0:T(1,128)S(1)}, s32[1,1,256]{2,1,0:T(1,128)}, u32[]{:S(2)}) %copy-start.6) | copy-done | bytes 1048
  6.0 0.0 copy-start.7
  6.0 0.7 %copy-done.7 = s32[1,1,256]{2,1,0:T(1,128)S(1)} copy-done((s32[1,1,256]{2,1,0:T(1,128)S(1)}, s32[1,1,256]{2,1,0:T(1,128)}, u32[]{:S(2)}) %copy-start.7) | copy-done | bytes 1048
  6.7 0.0 copy-start.8
  6.7 0.7 %copy-done.8 = s32[1,1,2]{2,1,0:T(1,128)S(1)} copy-done((s32[1,1,2]{2,1,0:T(1,128)S(1)}, s32[1,1,2]{2,1,0:T(1,128)}, u32[]{:S(2)}) %copy-start.8) | copy-done | bytes 32
  7.4 28.1 %patch_attention_grad.1 = bf16[1,256,512]{2,1,0:T(8,128)(2,1)S(1)} custom-call(bf16[1,256,512]{2,1,0:T(8,128)(2,1)S(1)} %copy-done.1, bf16[1,256,512]{2,1,0:T(8,128)(2,1)S(1)} %copy-done.2, bf16[1,512,768]{2,1,0:T(8,128)(2,1)S(1)} %copy-done, bf16[1,256,512]{2,1,0:T(8,128)(2,1)S(1)} %copy-done.3, f32[1,512]{1,0:T(1,128)S(1)} %copy-done.4, ...), custom_call_target="tpu_custom_call" | custom-call | tf_op jit(solution)/shard_map/patch_attention_grad/pallas_call | solution.py:303
  35.4 0.7 %copy.11 = bf16[1,256,512]{2,1,0:T(8,128)(2,1)} copy(bf16[1,256,512]{2,1,0:T(8,128)(2,1)S(1)} %patch_attention_grad.1) | data formatting | bytes 524288
Async XLA Ops:
  0.0 1.1 %copy-start = (bf16[1,512,768]{2,1,0:T(8,128)(2,1)S(1)}, bf16[1,512,768]{2,1,0:T(8,128)(2,1)}, u32[]{:S(2)}) copy-start(bf16[1,512,768]{2,1,0:T(8,128)(2,1)} %w_ref.1) | copy-start | bytes 2359300
  1.1 0.9 %copy-start.1 = (bf16[1,256,512]{2,1,0:T(8,128)(2,1)S(1)}, bf16[1,256,512]{2,1,0:T(8,128)(2,1)}, u32[]{:S(2)}) copy-start(bf16[1,256,512]{2,1,0:T(8,128)(2,1)} %x_ref.1) | copy-start | bytes 786436
  2.1 0.9 %copy-start.2 = (bf16[1,256,512]{2,1,0:T(8,128)(2,1)S(1)}, bf16[1,256,512]{2,1,0:T(8,128)(2,1)}, u32[]{:S(2)}) copy-start(bf16[1,256,512]{2,1,0:T(8,128)(2,1)} %up_ref.1) | copy-start | bytes 786436
  3.0 0.9 %copy-start.3 = (bf16[1,256,512]{2,1,0:T(8,128)(2,1)S(1)}, bf16[1,256,512]{2,1,0:T(8,128)(2,1)}, u32[]{:S(2)}) copy-start(bf16[1,256,512]{2,1,0:T(8,128)(2,1)} %wo_ref.1) | copy-start | bytes 786436
  4.0 0.7 %copy-start.4 = (f32[1,512]{1,0:T(1,128)S(1)}, f32[1,512]{1,0:T(1,128)}, u32[]{:S(2)}) copy-start(f32[1,512]{1,0:T(1,128)} %gain_ref.1) | copy-start | bytes 6148
  4.7 0.7 %copy-start.5 = (f32[1,512]{1,0:T(1,128)S(1)}, f32[1,512]{1,0:T(1,128)}, u32[]{:S(2)}) copy-start(f32[1,512]{1,0:T(1,128)} %bias_ref.1) | copy-start | bytes 6148
  5.3 0.7 %copy-start.6 = (s32[1,1,256]{2,1,0:T(1,128)S(1)}, s32[1,1,256]{2,1,0:T(1,128)}, u32[]{:S(2)}) copy-start(s32[1,1,256]{2,1,0:T(1,128)} %send_ref.1) | copy-start | bytes 3076
  6.0 0.7 %copy-start.7 = (s32[1,1,256]{2,1,0:T(1,128)S(1)}, s32[1,1,256]{2,1,0:T(1,128)}, u32[]{:S(2)}) copy-start(s32[1,1,256]{2,1,0:T(1,128)} %recv_ref.1) | copy-start | bytes 3076
  6.7 0.7 %copy-start.8 = (s32[1,1,2]{2,1,0:T(1,128)S(1)}, s32[1,1,2]{2,1,0:T(1,128)}, u32[]{:S(2)}) copy-start(s32[1,1,2]{2,1,0:T(1,128)} %len_ref.1) | copy-start | bytes 28

commit v2 on v1

--- a/solution.py
+++ b/solution.py
@@ -24,12 +24,16 @@
 
 def each(first, count, body):
     if count - first <= 8:
-        for step in range(first, count):
+        for step in by_distance(first, count):
             body(step)
     else:
         lax.fori_loop(first, count, lambda step, carry: (body(step), carry)[1], 0)
 
 
+def by_distance(first, count):
+    return sorted(range(first, count), key=lambda step: (abs(step - count // 2), step))
+
+
 def iota(shape, axis):
     return lax.broadcasted_iota(jnp.int32, shape, axis)
 
@@ -37,6 +41,16 @@
 def kernel(
     n,
     sections,
+    x_hbm,
+    up_hbm,
+    w_hbm,
+    wo_hbm,
+    gain_hbm,
+    bias_hbm,
+    send_hbm,
+    recv_hbm,
+    len_hbm,
+    out_ref,
     x_ref,
     up_ref,
     w_ref,
@@ -46,7 +60,7 @@
     send_ref,
     recv_ref,
     len_ref,
-    out_ref,
+    load_sem,
     send_x,
     recv_x,
     send_o,
@@ -65,6 +79,9 @@
     feat_q,
     feat_k,
     dqt_ref,
+    probs_ref,
+    dqkv_ref,
+    inverse_ref,
     dk_ref,
     dv_ref,
     sx_sem,
@@ -130,10 +147,29 @@
             device_id=(me, section - 1), device_id_type=MESH,
         )
 
+    loads = [
+        pltpu.make_async_copy(source, target, load_sem.at[i])
+        for i, (source, target) in enumerate(
+            [
+                (x_hbm, x_ref),
+                (up_hbm, up_ref),
+                (w_hbm, w_ref),
+                (wo_hbm, wo_ref),
+                (gain_hbm, gain_ref),
+                (bias_hbm, bias_ref),
+                (send_hbm, send_ref),
+                (recv_hbm, recv_ref),
+                (len_hbm, len_ref),
+            ]
+        )
+    ]
     barrier = pltpu.get_barrier_semaphore()
 
     @pl.when(section > 0)
     def _():
+        for i in (6, 0, 3, 1, 7, 8, 4, 5, 2):
+            loads[i].start()
+
         def greet(step):
             pl.semaphore_signal(
                 barrier, inc=1, device_id=(lax.rem(me + step, n), section), device_id_type=MESH
@@ -152,14 +188,18 @@
 
     @pl.when(section > 0)
     def _():
+        loads[6].wait()
         order_own[...] = jnp.broadcast_to(send_ref[0], order_own.shape)
         row_of = send_ref[0].astype(jnp.float32)
         eye = iota((rows, rows), 0) == iota((rows, rows), 1)
         column = jnp.sum(jnp.where(eye, row_of, 0.0), axis=1, keepdims=True).astype(jnp.int32)
         pick = jnp.where(column == iota((rows, rows), 1), 1.0, 0.0).astype(jnp.bfloat16)
+        loads[0].wait()
         send_x[...] = spread(dot(pick, x_ref[0]).astype(jnp.bfloat16))
         pl.semaphore_wait(barrier, 2 * n - 1)
         each(1, n, lambda step: x_copy(lax.rem(me + step, n), me, lax.rem(me + step, n)).start())
+        loads[1].wait()
+        loads[3].wait()
         out_common = dot_nt(up_ref[0], wo_ref[0]).astype(jnp.bfloat16)
         send_o[...] = spread(dot(pick, out_common).astype(jnp.bfloat16))
         each(1, n, lambda step: o_copy(lax.rem(me + step, n), me, lax.rem(me + step, n)).start())
@@ -168,11 +208,13 @@
         recv_x[me] = send_x[me]
         recv_o[me] = send_o[me]
 
+        loads[7].wait()
+        loads[8].wait()
         place = iota((1, rows), 1)
-        end = jnp.int32(0)
+        end = jnp.zeros((1, 1), jnp.int32)
         segment = jnp.zeros((1, rows), jnp.float32)
         for patch in range(len_ref.shape[2]):
-            end = end + len_ref[0, 0, patch]
+            end = end + len_ref[0, :, patch : patch + 1]
             segment = segment + jnp.where(place >= end, 1.0, 0.0)
         at = recv_ref[0] == iota((rows, rows), 0)
         patch_of = jnp.sum(jnp.where(at, segment, 0.0), axis=1, keepdims=True).astype(jnp.int32)
@@ -180,6 +222,9 @@
         feat_k[...] = jnp.where(patch_of == lanes, 1.0, 0.0).astype(jnp.bfloat16)
         feat_q[...] = jnp.where(patch_of == lanes, 0.0, -1e30).astype(jnp.bfloat16)
 
+        for i in (4, 5, 2):
+            loads[i].wait()
+
         def x_wait(step):
             peer = lax.rem(me + step, n)
             x_copy(peer, peer, peer).wait_recv()
@@ -190,6 +235,7 @@
         inverse = lax.rsqrt(jnp.mean(centered * centered, axis=-1, keepdims=True) + 1e-05)
         xhat = centered * inverse
         xhat_ref[...] = xhat
+        inverse_ref[...] = jnp.broadcast_to(inverse, inverse_ref.shape)
         normed = (xhat * gain_ref[...] + bias_ref[...]).astype(jnp.bfloat16)
         q_ref[...] = dot(normed, w_ref[0, :, :width]).astype(jnp.bfloat16)
         key = dot(normed, w_ref[0, :, width : 2 * width]).astype(jnp.bfloat16)
@@ -197,63 +243,89 @@
         kt_ref[...] = key.astype(jnp.float32).T.astype(jnp.bfloat16)
         v_ref[...] = dot(normed, w_ref[0, :, 2 * width :]).astype(jnp.bfloat16)
 
+        rate = float(HEAD) ** (-0.5) * math.log2(math.e)
+        lane_head = iota((rows, half), 1) // HEAD
+        zero = jnp.zeros((rows, half), jnp.bfloat16)
+        groups = half // HEAD // GROUP
+
+        def softmax_heads(part, group):
+            columns = slice(part * half, (part + 1) * half)
+            query_right = jnp.concatenate([q_ref[:, columns], feat_q[...]], axis=1)
+            mine = [lane_head == group * GROUP + i for i in range(GROUP)]
+            key, feature = k_ref[:, columns], feat_k[...]
+            keys = jnp.concatenate(
+                [jnp.concatenate([jnp.where(m, key, zero), feature], axis=1) for m in mine], axis=0
+            )
+            scores = dot_nt(keys, query_right)
+            for i in range(GROUP):
+                score = scores[i * rows : (i + 1) * rows]
+                expo = jnp.exp2((score - jnp.max(score, axis=0, keepdims=True)) * rate)
+                start = pl.multiple_of(((part * groups + group) * GROUP + i) * rows, rows)
+                probs_ref[pl.ds(start, rows), :] = expo * (1.0 / jnp.sum(expo, axis=0, keepdims=True))
+
+        def gradient_heads(part, group):
+            columns = slice(part * half, (part + 1) * half)
+            query, value, dout = q_ref[:, columns], v_ref[:, columns], do_ref[:, columns]
+            mine = [lane_head == group * GROUP + i for i in range(GROUP)]
+            values = jnp.concatenate([jnp.where(m, value, zero) for m in mine], axis=0)
+            dprobs = dot_nt(values, dout)
+            weights, dscores = [], []
+            for i in range(GROUP):
+                start = pl.multiple_of(((part * groups + group) * GROUP + i) * rows, rows)
+                probs = probs_ref[pl.ds(start, rows), :]
+                dprob = dprobs[i * rows : (i + 1) * rows]
+                inner = jnp.sum(dprob * probs, axis=0, keepdims=True)
+                weights.append(probs.astype(jnp.bfloat16))
+                dscores.append((probs * (dprob - inner)).astype(jnp.bfloat16))
+            dkeys = dot(jnp.concatenate(dscores, axis=0), query)
+            dvalues = dot(jnp.concatenate(weights, axis=0), dout)
+            dkey, dvalue = dk_ref[:, columns], dv_ref[:, columns]
+            for i in range(GROUP):
+                dkey = jnp.where(mine[i], dkeys[i * rows : (i + 1) * rows], dkey)
+                dvalue = jnp.where(mine[i], dvalues[i * rows : (i + 1) * rows], dvalue)
+                start = pl.multiple_of(part * half + (group * GROUP + i) * HEAD, HEAD)
+                dqt_ref[pl.ds(start, HEAD), :] = dot(kt_ref[pl.ds(start, HEAD), :], dscores[i])
+            dk_ref[:, columns] = dkey
+            dv_ref[:, columns] = dvalue
+
+        def all_heads(some_heads):
+            for part in range(width // half):
+                lax.fori_loop(0, groups, lambda group, carry: (some_heads(part, group), carry)[1], 0)
+
+        all_heads(softmax_heads)
+
         def o_wait(step):
             peer = lax.rem(me + step, n)
             o_copy(peer, peer, peer).wait_recv()
 
         each(1, n, o_wait)
         do_ref[...] = gather(recv_o[...])
-
-        rate = float(HEAD) ** (-0.5) * math.log2(math.e)
-        lane_head = iota((rows, half), 1) // HEAD
-        zero = jnp.zeros((rows, half), jnp.bfloat16)
-        for part in range(width // half):
-            columns = slice(part * half, (part + 1) * half)
-
-            def some_heads(group, carry, columns=columns, part=part):
-                query, key, value, dout = q_ref[:, columns], k_ref[:, columns], v_ref[:, columns], do_ref[:, columns]
-                query_right = jnp.concatenate([query, feat_q[...]], axis=1)
-                mine = [lane_head == group * GROUP + i for i in range(GROUP)]
-                keys = jnp.concatenate(
-                    [jnp.concatenate([jnp.where(m, key, zero), feat_k[...]], axis=1) for m in mine], axis=0
-                )
-                values = jnp.concatenate([jnp.where(m, value, zero) for m in mine], axis=0)
-                scores = dot_nt(keys, query_right)
-                dprobs = dot_nt(values, dout)
-                weights, dscores = [], []
-                for i in range(GROUP):
-                    score = scores[i * rows : (i + 1) * rows]
-                    dprob = dprobs[i * rows : (i + 1) * rows]
-                    expo = jnp.exp2((score - jnp.max(score, axis=0, keepdims=True)) * rate)
-                    probs = expo * (1.0 / jnp.sum(expo, axis=0, keepdims=True))
-                    inner = jnp.sum(dprob * probs, axis=0, keepdims=True)
-                    weights.append(probs.astype(jnp.bfloat16))
-                    dscores.append((probs * (dprob - inner)).astype(jnp.bfloat16))
-                dkeys = dot(jnp.concatenate(dscores, axis=0), query)
-                dvalues = dot(jnp.concatenate(weights, axis=0), dout)
-                dkey, dvalue = dk_ref[:, columns], dv_ref[:, columns]
-                for i in range(GROUP):
-                    dkey = jnp.where(mine[i], dkeys[i * rows : (i + 1) * rows], dkey)
-                    dvalue = jnp.where(mine[i], dvalues[i * rows : (i + 1) * rows], dvalue)
-                    start = pl.multiple_of(part * half + (group * GROUP + i) * HEAD, HEAD)
-                    dqt_ref[pl.ds(start, HEAD), :] = dot(kt_ref[pl.ds(start, HEAD), :], dscores[i])
-                dk_ref[:, columns] = dkey
-                dv_ref[:, columns] = dvalue
-                return carry
-
-            lax.fori_loop(0, half // HEAD // GROUP, some_heads, 0)
+        all_heads(gradient_heads)
 
         scale = float(HEAD) ** (-0.5)
-        dquery = (dqt_ref[...].T * scale).astype(jnp.bfloat16)
-        dkey = (dk_ref[...] * scale).astype(jnp.bfloat16)
-        dqkv = jnp.concatenate([dquery, dkey, dv_ref[...].astype(jnp.bfloat16)], axis=1)
-        grad = dot_nt(dqkv, w_ref[0]) * gain_ref[...]
-        xhat = xhat_ref[...]
-        mean = jnp.mean(grad, axis=-1, keepdims=True)
-        cross = jnp.mean(grad * xhat, axis=-1, keepdims=True)
-        branch = inverse * (grad - mean - xhat * cross)
-        send_b[...] = spread(branch.astype(jnp.bfloat16))
-        each(0, n, lambda step: b_copy(lax.rem(me + step, n), me, lax.rem(me + step, n)).start())
+        dqkv_ref[:, :width] = (dqt_ref[...].T * scale).astype(jnp.bfloat16)
+        dqkv_ref[:, width : 2 * width] = (dk_ref[...] * scale).astype(jnp.bfloat16)
+        dqkv_ref[:, 2 * width :] = dv_ref[...].astype(jnp.bfloat16)
+        pieces = 2 if slot == block and n % 2 == 0 else 1
+        peers, few = n // pieces, rows // pieces
+        for piece in range(pieces):
+            which = lax.rem(me // peers + 1 + piece, pieces)
+            some = pl.ds(pl.multiple_of(which * few, few), few)
+            grad = dot_nt(dqkv_ref[some, :], w_ref[0]) * gain_ref[...]
+            xhat = xhat_ref[some, :]
+            mean = jnp.mean(grad, axis=-1, keepdims=True)
+            cross = jnp.mean(grad * xhat, axis=-1, keepdims=True)
+            branch = (inverse_ref[some, :1] * (grad - mean - xhat * cross)).astype(jnp.bfloat16)
+            if pieces == 1:
+                send_b[...] = spread(branch)
+            else:
+                send_b[pl.ds(which * peers, peers)] = branch.reshape(peers, slot, wide)
+
+            def send_back(step, which=which):
+                peer = which * peers + lax.rem(me + step, peers)
+                b_copy(peer, me, peer).start()
+
+            each(0, peers, send_back)
 
     @pl.when(section < sections - 1)
     def _():
@@ -297,15 +369,17 @@
     width = w_out.shape[1]
     slot = max(rows // n, 16)
     vmem = pl.BlockSpec(memory_space=pltpu.VMEM)
-    smem = pl.BlockSpec(memory_space=pltpu.SMEM)
     bf16, f32 = jnp.bfloat16, jnp.float32
     dma = pltpu.SemaphoreType.DMA
+    operands = (x, up, w_qkv, w_out, gain, bias, send_order, recv_order, lengths)
     return pl.pallas_call(
         functools.partial(kernel, n, sections),
         out_shape=jax.ShapeDtypeStruct(x.shape, bf16),
-        in_specs=[vmem] * 8 + [smem],
+        in_specs=[pl.BlockSpec(memory_space=pltpu.HBM)] * 9,
         out_specs=vmem,
         scratch_shapes=[
+            *[pltpu.VMEM(a.shape, a.dtype) for a in operands],
+            dma((len(operands),)),
             pltpu.VMEM((n, slot, wide), bf16),
             pltpu.VMEM((n, slot, wide), bf16),
             pltpu.VMEM((n, slot, width), bf16),
@@ -324,6 +398,9 @@
             pltpu.VMEM((rows, 128), bf16),
             pltpu.VMEM((rows, 128), bf16),
             pltpu.VMEM((width, rows), f32),
+            pltpu.VMEM((width // HEAD * rows, rows), f32),
+            pltpu.VMEM((rows, 3 * width), bf16),
+            pltpu.VMEM((rows, 128), f32),
             pltpu.VMEM((rows, width), f32),
             pltpu.VMEM((rows, width), f32),
             dma((n,)),
@@ -336,10 +413,10 @@
             dma((2,)),
         ],
         compiler_params=pltpu.CompilerParams(
-            collective_id=0, has_side_effects=True, vmem_limit_bytes=40 * 1024 * 1024
+            collective_id=0, has_side_effects=True, vmem_limit_bytes=62 * 1024 * 1024
         ),
         name="patch_attention_grad",
-    )(x, up, w_qkv, w_out, gain, bias, send_order, recv_order, lengths)
+    )(*operands)
 
 
 def solution(mesh):

time: 36.5 us -> 31.2 us (0.85)
  local copies, waits for them, and re-layouts: 8.06 us -> 1.67 us
  Pallas kernels: 28.1 us -> 29.4 us
    unnamed x19 -> x1, local copies, waits for them, and re-layouts: 8.06 us -> 1.67 us
    pallas_call x1, Pallas kernels: 28.1 us -> 29.4 us  [per_device(): pl.pallas_call(functools.partial(kernel, n, sections), out_shape=jax.Shap...]
where the time goes in v2:
time: 31.2 us; the launch traced here: 31.1 us
  Pallas kernels  29.4 us (94%)
  local copies, waits for them, and re-layouts  1.67 us (5%)
    pallas_call x1, Pallas kernels, per_device(): pl.pallas_call(functools.partial(kernel, n, sections), out_shape=jax.Shap...  29.4 us
    unnamed x1, local copies, waits for them, and re-layouts  1.67 us

profile of v2, /device:TPU:1, one launch (start us, length us, event | category | flops | bytes accessed | tf_op | source)
XLA Modules:
  0.0 31.1 jit_solution(9662710964004166305)
XLA Ops:
  0.0 29.4 %patch_attention_grad.1 = bf16[1,256,512]{2,1,0:T(8,128)(2,1)} custom-call(bf16[1,256,512]{2,1,0:T(8,128)(2,1)} %x_hbm.1, bf16[1,256,512]{2,1,0:T(8,128)(2,1)} %up_hbm.1, bf16[1,512,768]{2,1,0:T(8,128)(2,1)} %w_hbm.1, bf16[1,256,512]{2,1,0:T(8,128)(2,1)} %wo_hbm.1, f32[1,512]{1,0:T(1,128)} %gain_hbm.1, f32[1,512]{1,0:T(1,128)} %bias_hbm.1, ...), custom_call_target="tpu_custom_call" | custom-call | tf_op jit(solution)/shard_map/patch_attention_grad/pallas_call | solution.py:375
  29.4 1.7 %copy.11 = bf16[1,256,512]{2,1,0:T(8,128)(2,1)} copy(bf16[1,256,512]{2,1,0:T(8,128)(2,1)} %patch_attention_grad.1) | data formatting | bytes 524288

commit v3 on v2

--- a/solution.py
+++ b/solution.py
@@ -372,6 +372,7 @@
     bf16, f32 = jnp.bfloat16, jnp.float32
     dma = pltpu.SemaphoreType.DMA
     operands = (x, up, w_qkv, w_out, gain, bias, send_order, recv_order, lengths)
+    operands = [pltpu.with_memory_space_constraint(a, pltpu.HBM) for a in operands]
     return pl.pallas_call(
         functools.partial(kernel, n, sections),
         out_shape=jax.ShapeDtypeStruct(x.shape, bf16),
@@ -413,7 +414,7 @@
             dma((2,)),
         ],
         compiler_params=pltpu.CompilerParams(
-            collective_id=0, has_side_effects=True, vmem_limit_bytes=62 * 1024 * 1024
+            collective_id=0, has_side_effects=True, vmem_limit_bytes=40 * 1024 * 1024
         ),
         name="patch_attention_grad",
     )(*operands)

time: 31.2 us -> 29.5 us (0.946)
  local copies, waits for them, and re-layouts: 1.67 us -> 0.71 us
  Pallas kernels: 29.4 us -> 28.7 us
    unnamed x1, local copies, waits for them, and re-layouts: 1.67 us -> 0.71 us
    pallas_call x1, Pallas kernels: 29.4 us -> 28.7 us  [per_device(): pl.pallas_call(functools.partial(kernel, n, sections), out_shape=jax.Shap...]
where the time goes in v3:
time: 29.5 us; the launch traced here: 29.4 us
  Pallas kernels  28.7 us (97%)
  local copies, waits for them, and re-layouts  0.71 us (2%)
    pallas_call x1, Pallas kernels, per_device(): pl.pallas_call(functools.partial(kernel, n, sections), out_shape=jax.Shap...  28.7 us
    unnamed x1, local copies, waits for them, and re-layouts  0.71 us

profile of v3, /device:TPU:1, one launch (start us, length us, event | category | flops | bytes accessed | tf_op | source)
XLA Modules:
  0.0 29.4 jit_solution(10878899366211663440)
XLA Ops:
  0.0 28.7 %patch_attention_grad.1 = bf16[1,256,512]{2,1,0:T(8,128)(2,1)S(1)} custom-call(bf16[1,256,512]{2,1,0:T(8,128)(2,1)} %x_hbm.1, bf16[1,256,512]{2,1,0:T(8,128)(2,1)} %up_hbm.1, bf16[1,512,768]{2,1,0:T(8,128)(2,1)} %w_hbm.1, bf16[1,256,512]{2,1,0:T(8,128)(2,1)} %wo_hbm.1, f32[1,512]{1,0:T(1,128)} %gain_hbm.1, f32[1,512]{1,0:T(1,128)} %bias_hbm.1, ...), custom_call_target="tpu_custom_call" | custom-call | tf_op jit(solution)/shard_map/patch_attention_grad/pallas_call | solution.py:376
  28.7 0.7 %copy.11 = bf16[1,256,512]{2,1,0:T(8,128)(2,1)} copy(bf16[1,256,512]{2,1,0:T(8,128)(2,1)S(1)} %patch_attention_grad.1) | data formatting | bytes 524288

commit v4 on v3

--- a/solution.py
+++ b/solution.py
@@ -41,6 +41,7 @@
 def kernel(
     n,
     sections,
+    paired,
     x_hbm,
     up_hbm,
     w_hbm,
@@ -92,6 +93,7 @@
     rb_sem,
     up_sem,
     order_sem,
+    turn_sem,
 ):
     me = lax.axis_index("seq")
     section = lax.axis_index("section")
@@ -186,6 +188,14 @@
 
         each(0, n, greet)
 
+    first_of_pair = (section % 2 == 0) & (section > 0)
+    second_of_pair = (section % 2 == 1) & (section > 1)
+    if paired:
+
+        @pl.when(second_of_pair)
+        def _():
+            pl.semaphore_signal(barrier, inc=1, device_id=(me, section - 1), device_id_type=MESH)
+
     @pl.when(section > 0)
     def _():
         loads[6].wait()
@@ -196,15 +206,21 @@
         pick = jnp.where(column == iota((rows, rows), 1), 1.0, 0.0).astype(jnp.bfloat16)
         loads[0].wait()
         send_x[...] = spread(dot(pick, x_ref[0]).astype(jnp.bfloat16))
-        pl.semaphore_wait(barrier, 2 * n - 1)
+        greetings = 2 * n - 1
+        if paired:
+            greetings = greetings + first_of_pair.astype(jnp.int32)
+        pl.semaphore_wait(barrier, greetings)
+        if paired:
+
+            @pl.when(second_of_pair)
+            def _():
+                pl.semaphore_wait(turn_sem, 1)
+
         each(1, n, lambda step: x_copy(lax.rem(me + step, n), me, lax.rem(me + step, n)).start())
         loads[1].wait()
         loads[3].wait()
         out_common = dot_nt(up_ref[0], wo_ref[0]).astype(jnp.bfloat16)
         send_o[...] = spread(dot(pick, out_common).astype(jnp.bfloat16))
-        each(1, n, lambda step: o_copy(lax.rem(me + step, n), me, lax.rem(me + step, n)).start())
-        up_copy().start()
-        order_copy().start()
         recv_x[me] = send_x[me]
         recv_o[me] = send_o[me]
 
@@ -225,6 +241,17 @@
         for i in (4, 5, 2):
             loads[i].wait()
 
+        def x_sent(step):
+            peer = lax.rem(me + step, n)
+            x_copy(peer, me, peer).wait_send()
+
+        each(1, n, x_sent)
+        if paired:
+
+            @pl.when(first_of_pair)
+            def _():
+                pl.semaphore_signal(turn_sem, inc=1, device_id=(me, section + 1), device_id_type=MESH)
+
         def x_wait(step):
             peer = lax.rem(me + step, n)
             x_copy(peer, peer, peer).wait_recv()
@@ -243,6 +270,10 @@
         kt_ref[...] = key.astype(jnp.float32).T.astype(jnp.bfloat16)
         v_ref[...] = dot(normed, w_ref[0, :, 2 * width :]).astype(jnp.bfloat16)
 
+        each(1, n, lambda step: o_copy(lax.rem(me + step, n), me, lax.rem(me + step, n)).start())
+        up_copy().start()
+        order_copy().start()
+
         rate = float(HEAD) ** (-0.5) * math.log2(math.e)
         lane_head = iota((rows, half), 1) // HEAD
         zero = jnp.zeros((rows, half), jnp.bfloat16)
@@ -258,10 +289,12 @@
             )
             scores = dot_nt(keys, query_right)
             for i in range(GROUP):
-                score = scores[i * rows : (i + 1) * rows]
-                expo = jnp.exp2((score - jnp.max(score, axis=0, keepdims=True)) * rate)
                 start = pl.multiple_of(((part * groups + group) * GROUP + i) * rows, rows)
-                probs_ref[pl.ds(start, rows), :] = expo * (1.0 / jnp.sum(expo, axis=0, keepdims=True))
+                for first in range(0, rows, half):
+                    some = slice(first, first + half)
+                    score = scores[i * rows : (i + 1) * rows, some]
+                    expo = jnp.exp2((score - jnp.max(score, axis=0, keepdims=True)) * rate)
+                    probs_ref[pl.ds(start, rows), some] = expo * (1.0 / jnp.sum(expo, axis=0, keepdims=True))
 
         def gradient_heads(part, group):
             columns = slice(part * half, (part + 1) * half)
@@ -272,11 +305,16 @@
             weights, dscores = [], []
             for i in range(GROUP):
                 start = pl.multiple_of(((part * groups + group) * GROUP + i) * rows, rows)
-                probs = probs_ref[pl.ds(start, rows), :]
-                dprob = dprobs[i * rows : (i + 1) * rows]
-                inner = jnp.sum(dprob * probs, axis=0, keepdims=True)
-                weights.append(probs.astype(jnp.bfloat16))
-                dscores.append((probs * (dprob - inner)).astype(jnp.bfloat16))
+                weight, dscore = [], []
+                for first in range(0, rows, half):
+                    some = slice(first, first + half)
+                    probs = probs_ref[pl.ds(start, rows), some]
+                    dprob = dprobs[i * rows : (i + 1) * rows, some]
+                    inner = jnp.sum(dprob * probs, axis=0, keepdims=True)
+                    weight.append(probs.astype(jnp.bfloat16))
+                    dscore.append((probs * (dprob - inner)).astype(jnp.bfloat16))
+                weights.append(jnp.concatenate(weight, axis=1))
+                dscores.append(jnp.concatenate(dscore, axis=1))
             dkeys = dot(jnp.concatenate(dscores, axis=0), query)
             dvalues = dot(jnp.concatenate(weights, axis=0), dout)
             dkey, dvalue = dk_ref[:, columns], dv_ref[:, columns]
@@ -349,7 +387,6 @@
     def _():
         def sent(step):
             peer = lax.rem(me + step, n)
-            x_copy(peer, me, peer).wait_send()
             o_copy(peer, me, peer).wait_send()
 
         each(1, n, sent)
@@ -374,7 +411,7 @@
     operands = (x, up, w_qkv, w_out, gain, bias, send_order, recv_order, lengths)
     operands = [pltpu.with_memory_space_constraint(a, pltpu.HBM) for a in operands]
     return pl.pallas_call(
-        functools.partial(kernel, n, sections),
+        functools.partial(kernel, n, sections, sections % 2 == 0 and n <= 8),
         out_shape=jax.ShapeDtypeStruct(x.shape, bf16),
         in_specs=[pl.BlockSpec(memory_space=pltpu.HBM)] * 9,
         out_specs=vmem,
@@ -412,6 +449,7 @@
             dma((n,)),
             dma((2,)),
             dma((2,)),
+            pltpu.SemaphoreType.REGULAR,
         ],
         compiler_params=pltpu.CompilerParams(
             collective_id=0, has_side_effects=True, vmem_limit_bytes=40 * 1024 * 1024

time: 29.5 us -> 30.5 us (1.034)
  Pallas kernels: 28.7 us -> 29.7 us
    pallas_call x1, Pallas kernels: 28.7 us -> 29.7 us  [per_device(): pl.pallas_call(functools.partial(kernel, n, sections, sections % 2 == 0 a...]
where the time goes in v4:
time: 30.5 us; the launch traced here: 30.4 us
  Pallas kernels  29.7 us (97%)
  local copies, waits for them, and re-layouts  0.71 us (2%)
    pallas_call x1, Pallas kernels, per_device(): pl.pallas_call(functools.partial(kernel, n, sections, sections % 2 == 0 a...  29.7 us
    unnamed x1, local copies, waits for them, and re-layouts  0.71 us

profile of v4, /device:TPU:1, one launch (start us, length us, event | category | flops | bytes accessed | tf_op | source)
XLA Modules:
  0.0 30.4 jit_solution(7676093534773021665)
XLA Ops:
  0.0 29.7 %patch_attention_grad.1 = bf16[1,256,512]{2,1,0:T(8,128)(2,1)S(1)} custom-call(bf16[1,256,512]{2,1,0:T(8,128)(2,1)} %x_hbm.1, bf16[1,256,512]{2,1,0:T(8,128)(2,1)} %up_hbm.1, bf16[1,512,768]{2,1,0:T(8,128)(2,1)} %w_hbm.1, bf16[1,256,512]{2,1,0:T(8,128)(2,1)} %wo_hbm.1, f32[1,512]{1,0:T(1,128)} %gain_hbm.1, f32[1,512]{1,0:T(1,128)} %bias_hbm.1, ...), custom_call_target="tpu_custom_call" | custom-call | tf_op jit(solution)/shard_map/patch_attention_grad/pallas_call | solution.py:413
  29.7 0.7 %copy.11 = bf16[1,256,512]{2,1,0:T(8,128)(2,1)} copy(bf16[1,256,512]{2,1,0:T(8,128)(2,1)S(1)} %patch_attention_grad.1) | data formatting | bytes 524288

commit v5 on v4

--- a/solution.py
+++ b/solution.py
@@ -149,6 +149,11 @@
             device_id=(me, section - 1), device_id_type=MESH,
         )
 
+    def x_sent(step):
+        peer = lax.rem(me + step, n)
+        x_copy(peer, me, peer).wait_send()
+
+    far = by_distance(1, n)[:5] if paired else []
     loads = [
         pltpu.make_async_copy(source, target, load_sem.at[i])
         for i, (source, target) in enumerate(
@@ -221,6 +226,9 @@
         loads[3].wait()
         out_common = dot_nt(up_ref[0], wo_ref[0]).astype(jnp.bfloat16)
         send_o[...] = spread(dot(pick, out_common).astype(jnp.bfloat16))
+        each(1, n, lambda step: o_copy(lax.rem(me + step, n), me, lax.rem(me + step, n)).start())
+        up_copy().start()
+        order_copy().start()
         recv_x[me] = send_x[me]
         recv_o[me] = send_o[me]
 
@@ -241,15 +249,12 @@
         for i in (4, 5, 2):
             loads[i].wait()
 
-        def x_sent(step):
-            peer = lax.rem(me + step, n)
-            x_copy(peer, me, peer).wait_send()
-
-        each(1, n, x_sent)
         if paired:
 
             @pl.when(first_of_pair)
             def _():
+                for step in far:
+                    x_sent(step)
                 pl.semaphore_signal(turn_sem, inc=1, device_id=(me, section + 1), device_id_type=MESH)
 
         def x_wait(step):
@@ -269,10 +274,6 @@
         k_ref[...] = key
         kt_ref[...] = key.astype(jnp.float32).T.astype(jnp.bfloat16)
         v_ref[...] = dot(normed, w_ref[0, :, 2 * width :]).astype(jnp.bfloat16)
-
-        each(1, n, lambda step: o_copy(lax.rem(me + step, n), me, lax.rem(me + step, n)).start())
-        up_copy().start()
-        order_copy().start()
 
         rate = float(HEAD) ** (-0.5) * math.log2(math.e)
         lane_head = iota((rows, half), 1) // HEAD
@@ -388,6 +389,13 @@
         def sent(step):
             peer = lax.rem(me + step, n)
             o_copy(peer, me, peer).wait_send()
+            if not paired or step not in far:
+                x_sent(step)
+            else:
+
+                @pl.when(jnp.logical_not(first_of_pair))
+                def _():
+                    x_sent(step)
 
         each(1, n, sent)
 

time: 30.5 us -> 27.7 us (0.908)
  the two profiles are of different devices: /device:TPU:1 before, /device:TPU:2 now
where the time goes in v5:
time: 27.7 us; the launch traced here: 27.6 us
  Pallas kernels  26.9 us (97%)
  local copies, waits for them, and re-layouts  0.71 us (3%)
    pallas_call x1, Pallas kernels, per_device(): pl.pallas_call(functools.partial(kernel, n, sections, sections % 2 == 0 a...  26.9 us
    unnamed x1, local copies, waits for them, and re-layouts  0.71 us

profile of v5, /device:TPU:2, one launch (start us, length us, event | category | flops | bytes accessed | tf_op | source)
XLA Modules:
  0.0 27.6 jit_solution(309399450951697181)
XLA Ops:
  0.0 26.9 %patch_attention_grad.1 = bf16[1,256,512]{2,1,0:T(8,128)(2,1)S(1)} custom-call(bf16[1,256,512]{2,1,0:T(8,128)(2,1)} %x_hbm.1, bf16[1,256,512]{2,1,0:T(8,128)(2,1)} %up_hbm.1, bf16[1,512,768]{2,1,0:T(8,128)(2,1)} %w_hbm.1, bf16[1,256,512]{2,1,0:T(8,128)(2,1)} %wo_hbm.1, f32[1,512]{1,0:T(1,128)} %gain_hbm.1, f32[1,512]{1,0:T(1,128)} %bias_hbm.1, ...), custom_call_target="tpu_custom_call" | custom-call | tf_op jit(solution)/shard_map/patch_attention_grad/pallas_call | solution.py:421
  26.9 0.7 %copy.11 = bf16[1,256,512]{2,1,0:T(8,128)(2,1)} copy(bf16[1,256,512]{2,1,0:T(8,128)(2,1)S(1)} %patch_attention_grad.1) | data formatting | bytes 524288

commit v6 on v5

--- a/solution.py
+++ b/solution.py
@@ -153,7 +153,7 @@
         peer = lax.rem(me + step, n)
         x_copy(peer, me, peer).wait_send()
 
-    far = by_distance(1, n)[:5] if paired else []
+    far = by_distance(1, n)[:3] if paired else []
     loads = [
         pltpu.make_async_copy(source, target, load_sem.at[i])
         for i, (source, target) in enumerate(
@@ -290,7 +290,7 @@
             )
             scores = dot_nt(keys, query_right)
             for i in range(GROUP):
-                start = pl.multiple_of(((part * groups + group) * GROUP + i) * rows, rows)
+                start = ((part * groups + group) * GROUP + i) * rows
                 for first in range(0, rows, half):
                     some = slice(first, first + half)
                     score = scores[i * rows : (i + 1) * rows, some]
@@ -305,7 +305,7 @@
             dprobs = dot_nt(values, dout)
             weights, dscores = [], []
             for i in range(GROUP):
-                start = pl.multiple_of(((part * groups + group) * GROUP + i) * rows, rows)
+                start = ((part * groups + group) * GROUP + i) * rows
                 weight, dscore = [], []
                 for first in range(0, rows, half):
                     some = slice(first, first + half)
@@ -322,14 +322,15 @@
             for i in range(GROUP):
                 dkey = jnp.where(mine[i], dkeys[i * rows : (i + 1) * rows], dkey)
                 dvalue = jnp.where(mine[i], dvalues[i * rows : (i + 1) * rows], dvalue)
-                start = pl.multiple_of(part * half + (group * GROUP + i) * HEAD, HEAD)
+                start = part * half + (group * GROUP + i) * HEAD
                 dqt_ref[pl.ds(start, HEAD), :] = dot(kt_ref[pl.ds(start, HEAD), :], dscores[i])
             dk_ref[:, columns] = dkey
             dv_ref[:, columns] = dvalue
 
         def all_heads(some_heads):
             for part in range(width // half):
-                lax.fori_loop(0, groups, lambda group, carry: (some_heads(part, group), carry)[1], 0)
+                for group in range(groups):
+                    some_heads(part, group)
 
         all_heads(softmax_heads)
 

time: 27.7 us -> 28.1 us (1.014)
  the two profiles are of different devices: /device:TPU:2 before, /device:TPU:1 now
where the time goes in v6:
time: 28.1 us; the launch traced here: 28 us
  Pallas kernels  27.3 us (97%)
  local copies, waits for them, and re-layouts  0.71 us (3%)
    pallas_call x1, Pallas kernels, per_device(): pl.pallas_call(functools.partial(kernel, n, sections, sections % 2 == 0 a...  27.3 us
    unnamed x1, local copies, waits for them, and re-layouts  0.71 us

profile of v6, /device:TPU:1, one launch (start us, length us, event | category | flops | bytes accessed | tf_op | source)
XLA Modules:
  0.0 28.0 jit_solution(7745357717146496323)
XLA Ops:
  0.0 27.3 %patch_attention_grad.1 = bf16[1,256,512]{2,1,0:T(8,128)(2,1)S(1)} custom-call(bf16[1,256,512]{2,1,0:T(8,128)(2,1)} %x_hbm.1, bf16[1,256,512]{2,1,0:T(8,128)(2,1)} %up_hbm.1, bf16[1,512,768]{2,1,0:T(8,128)(2,1)} %w_hbm.1, bf16[1,256,512]{2,1,0:T(8,128)(2,1)} %wo_hbm.1, f32[1,512]{1,0:T(1,128)} %gain_hbm.1, f32[1,512]{1,0:T(1,128)} %bias_hbm.1, ...), custom_call_target="tpu_custom_call" | custom-call | tf_op jit(solution)/shard_map/patch_attention_grad/pallas_call | solution.py:422
  27.3 0.7 %copy.11 = bf16[1,256,512]{2,1,0:T(8,128)(2,1)} copy(bf16[1,256,512]{2,1,0:T(8,128)(2,1)S(1)} %patch_attention_grad.1) | data formatting | bytes 524288

commit v7 on v6

--- a/solution.py
+++ b/solution.py
@@ -153,7 +153,7 @@
         peer = lax.rem(me + step, n)
         x_copy(peer, me, peer).wait_send()
 
-    far = by_distance(1, n)[:3] if paired else []
+    far = by_distance(1, n)[:5] if paired else []
     loads = [
         pltpu.make_async_copy(source, target, load_sem.at[i])
         for i, (source, target) in enumerate(

time: 28.1 us -> 26.7 us (0.950)
  Pallas kernels: 27.3 us -> 25.8 us
    pallas_call x1, Pallas kernels: 27.3 us -> 25.8 us  [per_device(): pl.pallas_call(functools.partial(kernel, n, sections, sections % 2 == 0 a...]
where the time goes in v7:
time: 26.7 us; the launch traced here: 26.6 us
  Pallas kernels  25.8 us (97%)
  local copies, waits for them, and re-layouts  0.71 us (3%)
    pallas_call x1, Pallas kernels, per_device(): pl.pallas_call(functools.partial(kernel, n, sections, sections % 2 == 0 a...  25.8 us
    unnamed x1, local copies, waits for them, and re-layouts  0.71 us

profile of v7, /device:TPU:1, one launch (start us, length us, event | category | flops | bytes accessed | tf_op | source)
XLA Modules:
  0.0 26.6 jit_solution(1150538317066427200)
XLA Ops:
  0.0 25.8 %patch_attention_grad.1 = bf16[1,256,512]{2,1,0:T(8,128)(2,1)S(1)} custom-call(bf16[1,256,512]{2,1,0:T(8,128)(2,1)} %x_hbm.1, bf16[1,256,512]{2,1,0:T(8,128)(2,1)} %up_hbm.1, bf16[1,512,768]{2,1,0:T(8,128)(2,1)} %w_hbm.1, bf16[1,256,512]{2,1,0:T(8,128)(2,1)} %wo_hbm.1, f32[1,512]{1,0:T(1,128)} %gain_hbm.1, f32[1,512]{1,0:T(1,128)} %bias_hbm.1, ...), custom_call_target="tpu_custom_call" | custom-call | tf_op jit(solution)/shard_map/patch_attention_grad/pallas_call | solution.py:422
  25.9 0.7 %copy.11 = bf16[1,256,512]{2,1,0:T(8,128)(2,1)} copy(bf16[1,256,512]{2,1,0:T(8,128)(2,1)S(1)} %patch_attention_grad.1) | data formatting | bytes 524288

commit v8 on v7

--- a/solution.py
+++ b/solution.py
@@ -11,7 +11,7 @@
 HEAD = 16
 MESH = pl.DeviceIdType.MESH
 LAST = (((1,), (1,)), ((), ()))
-GROUP = 4
+GROUP = 8
 
 
 def dot(a, b):

time: 26.7 us -> 26.3 us (0.985)
  Pallas kernels: 25.8 us -> 25.5 us
    pallas_call x1, Pallas kernels: 25.8 us -> 25.5 us  [per_device(): pl.pallas_call(functools.partial(kernel, n, sections, sections % 2 == 0 a...]
where the time goes in v8:
time: 26.3 us; the launch traced here: 26.2 us
  Pallas kernels  25.5 us (97%)
  local copies, waits for them, and re-layouts  0.71 us (3%)
    pallas_call x1, Pallas kernels, per_device(): pl.pallas_call(functools.partial(kernel, n, sections, sections % 2 == 0 a...  25.5 us
    unnamed x1, local copies, waits for them, and re-layouts  0.71 us

profile of v8, /device:TPU:1, one launch (start us, length us, event | category | flops | bytes accessed | tf_op | source)
XLA Modules:
  0.0 26.2 jit_solution(6590907994110418250)
XLA Ops:
  0.0 25.5 %patch_attention_grad.1 = bf16[1,256,512]{2,1,0:T(8,128)(2,1)S(1)} custom-call(bf16[1,256,512]{2,1,0:T(8,128)(2,1)} %x_hbm.1, bf16[1,256,512]{2,1,0:T(8,128)(2,1)} %up_hbm.1, bf16[1,512,768]{2,1,0:T(8,128)(2,1)} %w_hbm.1, bf16[1,256,512]{2,1,0:T(8,128)(2,1)} %wo_hbm.1, f32[1,512]{1,0:T(1,128)} %gain_hbm.1, f32[1,512]{1,0:T(1,128)} %bias_hbm.1, ...), custom_call_target="tpu_custom_call" | custom-call | tf_op jit(solution)/shard_map/patch_attention_grad/pallas_call | solution.py:422
  25.5 0.7 %copy.11 = bf16[1,256,512]{2,1,0:T(8,128)(2,1)} copy(bf16[1,256,512]{2,1,0:T(8,128)(2,1)S(1)} %patch_attention_grad.1) | data formatting | bytes 524288

commit v9 on v8

--- a/solution.py
+++ b/solution.py
@@ -257,23 +257,32 @@
                     x_sent(step)
                 pl.semaphore_signal(turn_sem, inc=1, device_id=(me, section + 1), device_id_type=MESH)
 
-        def x_wait(step):
-            peer = lax.rem(me + step, n)
-            x_copy(peer, peer, peer).wait_recv()
-
-        each(1, n, x_wait)
-        values = gather(recv_x[...]).astype(jnp.float32)
-        centered = values - jnp.mean(values, axis=-1, keepdims=True)
-        inverse = lax.rsqrt(jnp.mean(centered * centered, axis=-1, keepdims=True) + 1e-05)
-        xhat = centered * inverse
-        xhat_ref[...] = xhat
-        inverse_ref[...] = jnp.broadcast_to(inverse, inverse_ref.shape)
-        normed = (xhat * gain_ref[...] + bias_ref[...]).astype(jnp.bfloat16)
-        q_ref[...] = dot(normed, w_ref[0, :, :width]).astype(jnp.bfloat16)
-        key = dot(normed, w_ref[0, :, width : 2 * width]).astype(jnp.bfloat16)
-        k_ref[...] = key
-        kt_ref[...] = key.astype(jnp.float32).T.astype(jnp.bfloat16)
-        v_ref[...] = dot(normed, w_ref[0, :, 2 * width :]).astype(jnp.bfloat16)
+        pieces = 2 if slot == block and n % 2 == 0 else 1
+        peers, few = n // pieces, rows // pieces
+        for piece in range(pieces):
+            which = lax.rem(me // peers + piece, pieces)
+            some = pl.ds(pl.multiple_of(which * few, few), few)
+
+            def x_wait(step, which=which):
+                peer = which * peers + lax.rem(me + step, peers)
+                x_copy(peer, peer, peer).wait_recv()
+
+            each(1 if piece == 0 else 0, peers, x_wait)
+            if pieces == 1:
+                values = gather(recv_x[...])
+            else:
+                values = recv_x[pl.ds(which * peers, peers)].reshape(few, wide)
+            values = values.astype(jnp.float32)
+            centered = values - jnp.mean(values, axis=-1, keepdims=True)
+            inverse = lax.rsqrt(jnp.mean(centered * centered, axis=-1, keepdims=True) + 1e-05)
+            xhat = centered * inverse
+            xhat_ref[some, :] = xhat
+            inverse_ref[some, :] = jnp.broadcast_to(inverse, (few, half))
+            normed = (xhat * gain_ref[...] + bias_ref[...]).astype(jnp.bfloat16)
+            q_ref[some, :] = dot(normed, w_ref[0, :, :width]).astype(jnp.bfloat16)
+            k_ref[some, :] = dot(normed, w_ref[0, :, width : 2 * width]).astype(jnp.bfloat16)
+            v_ref[some, :] = dot(normed, w_ref[0, :, 2 * width :]).astype(jnp.bfloat16)
+        kt_ref[...] = k_ref[...].astype(jnp.float32).T.astype(jnp.bfloat16)
 
         rate = float(HEAD) ** (-0.5) * math.log2(math.e)
         lane_head = iota((rows, half), 1) // HEAD
@@ -346,8 +355,6 @@
         dqkv_ref[:, :width] = (dqt_ref[...].T * scale).astype(jnp.bfloat16)
         dqkv_ref[:, width : 2 * width] = (dk_ref[...] * scale).astype(jnp.bfloat16)
         dqkv_ref[:, 2 * width :] = dv_ref[...].astype(jnp.bfloat16)
-        pieces = 2 if slot == block and n % 2 == 0 else 1
-        peers, few = n // pieces, rows // pieces
         for piece in range(pieces):
             which = lax.rem(me // peers + 1 + piece, pieces)
             some = pl.ds(pl.multiple_of(which * few, few), few)

time: 26.3 us -> 26.4 us (level)
  no operation moved by 1% of the time
where the time goes in v9:
time: 26.4 us; the launch traced here: 26.3 us
  Pallas kernels  25.6 us (97%)
  local copies, waits for them, and re-layouts  0.71 us (3%)
    pallas_call x1, Pallas kernels, per_device(): pl.pallas_call(functools.partial(kernel, n, sections, sections % 2 == 0 a...  25.6 us
    unnamed x1, local copies, waits for them, and re-layouts  0.71 us

profile of v9, /device:TPU:1, one launch (start us, length us, event | category | flops | bytes accessed | tf_op | source)
XLA Modules:
  0.0 26.3 jit_solution(10424536231485857853)
XLA Ops:
  0.0 25.6 %patch_attention_grad.1 = bf16[1,256,512]{2,1,0:T(8,128)(2,1)S(1)} custom-call(bf16[1,256,512]{2,1,0:T(8,128)(2,1)} %x_hbm.1, bf16[1,256,512]{2,1,0:T(8,128)(2,1)} %up_hbm.1, bf16[1,512,768]{2,1,0:T(8,128)(2,1)} %w_hbm.1, bf16[1,256,512]{2,1,0:T(8,128)(2,1)} %wo_hbm.1, f32[1,512]{1,0:T(1,128)} %gain_hbm.1, f32[1,512]{1,0:T(1,128)} %bias_hbm.1, ...), custom_call_target="tpu_custom_call" | custom-call | tf_op jit(solution)/shard_map/patch_attention_grad/pallas_call | solution.py:429
  25.6 0.7 %copy.11 = bf16[1,256,512]{2,1,0:T(8,128)(2,1)} copy(bf16[1,256,512]{2,1,0:T(8,128)(2,1)S(1)} %patch_attention_grad.1) | data formatting | bytes 524288
